TPU v7x, 32 devices: a whole 2x2x4 slice. The times are simulated.
32 devices in a mesh: dp: 2 (over x), head: 1, row: 16 (over z, y, core).
Axes of the slice: x: 2, y: 2, z: 4, core: 2. Of those that a mesh axis runs over, the one named last changes fastest.
Arguments:
- pair_act: bfloat16 [256, 128, 128], P(('dp', 'row')), parts along dimension 0, may hold values from -12 to 12
- chain_id: int32 [256], P('dp'), parts along dimension 0, may hold values from 0 to 3, never falling along the last dimension, each value on 1 to 64 neighbouring positions
- residue_mask: int32 [256], P('dp'), parts along dimension 0, may hold values 0 or 1
- norm_gain: float32 [128], replicated, may hold values from 0.5 to 1.5
- w_proj: bfloat16 [128, 4, 128], P(None, 'head'), may hold values from -1.25 to 1.25
- w_bias: bfloat16 [128, 4], P(None, 'head'), may hold values from -0.9 to 0.9
- chain_bias: float32 [2, 4], P(None, 'head'), may hold values from -2 to 2
- w_out: bfloat16 [4, 32, 128], P('head'), may hold values from -0.5 to 0.5
- w_dist: bfloat16 [128, 64], replicated, may hold values from -0.5 to 0.5
- dist_bias: float32 [64], replicated, may hold values from -3 to 3
Outputs:
- new_pair: bfloat16 [256, 128, 128], P(('dp', 'row')), parts along dimension 0
- distogram: bfloat16 [256, 128, 64], P(('dp', 'row')), parts along dimension 0
There are 2 independent parts, one for each index of `dp`. A program takes and returns all parts, laid end to end along the dimension named above; an argument that names none is the same for every part. Nothing has to cross between parts.
Inputs may be any that keep to these rules, and one draw needn't show every extreme that they name: `chain_id`: chain ids never fall along the residues; no chain has more than half of the 128 residues.
All inputs are finite; a program needn't handle non-finite values.
Results may differ from a plain program's by a relative error of at most 0.013.
Values may be sent and summed in bfloat16 or wider, within the bound.
No kernel may reach another device: no remote copies, remote signals or barrier semaphores. Data moves between devices by JAX's collectives and lax.ppermute only.
A program may use at most 64 MiB of HBM per device.

v0:
```python
import functools

import jax
import jax.numpy as jnp
from jax import lax
from jax.experimental import pallas as pl
from jax.experimental.pallas import tpu as pltpu
from jax.sharding import PartitionSpec as P

LANES = 128
F32 = jnp.float32
BF16 = jnp.bfloat16
LOG2E = 1.4426950408889634


def dot_nt(a, b):
    return lax.dot_general(a, b, (((1,), (1,)), ((), ())), preferred_element_type=F32)


def dot_tn(a, b):
    return lax.dot_general(a, b, (((0,), (0,)), ((), ())), preferred_element_type=F32)


def dot_nn(a, b):
    return jnp.dot(a, b, preferred_element_type=F32)


def centring(chan):
    row = lax.broadcasted_iota(jnp.int32, (2 * chan, 2 * chan), 0)
    col = lax.broadcasted_iota(jnp.int32, (2 * chan, 2 * chan), 1)
    inside = (row // chan) == (col // chan)
    return (jnp.where(row == col, 1.0, 0.0) - jnp.where(inside, 1.0 / chan, 0.0)).astype(BF16)


def layer_norm(values, centre, gain):
    chan = gain.shape[1]
    centered = dot_nn(values, centre)
    halves = []
    for part in (centered[:, :chan], centered[:, chan:]):
        variance = jnp.mean(part * part, -1, keepdims=True)
        halves.append((part * lax.rsqrt(variance + 1e-05) * gain).astype(BF16))
    return halves


def swap_matrix(rows):
    size = 2 * rows * rows
    out = lax.broadcasted_iota(jnp.int32, (size, size), 0)
    col = lax.broadcasted_iota(jnp.int32, (size, size), 1)
    b, rest = out // (2 * rows), out % (2 * rows)
    wanted = (rest // rows) * (rows * rows) + (rest % rows) * rows + b
    return jnp.where(col == wanted, 1.0, 0.0).astype(BF16)


def pack_kernel(x_hbm, gain_hbm, wb_hbm, out_hbm, x_ref, gain_ref, wb_ref, out_ref, sems, out_sems):
    rows, n, chan = x_ref.shape
    peers = n // rows
    heads = wb_ref.shape[0]
    half = heads * rows // 2
    base = rows * rows
    fetch_gain = pltpu.make_async_copy(gain_hbm, gain_ref, sems.at[rows])
    fetch_wb = pltpu.make_async_copy(wb_hbm, wb_ref, sems.at[rows + 1])
    fetches = [pltpu.make_async_copy(x_hbm.at[k], x_ref.at[k], sems.at[k]) for k in range(rows)]
    for copy in (fetch_gain, fetch_wb, *fetches):
        copy.start()
    stores = []

    def store(first, count):
        at = pl.ds(first, count)
        copy = pltpu.make_async_copy(out_ref.at[:, at, :], out_hbm.at[:, at, :], out_sems.at[len(stores)])
        copy.start()
        stores.append(copy)

    centre = centring(chan)
    owner = lax.broadcasted_iota(jnp.int32, (heads * rows, chan), 0) % rows
    bias = jnp.zeros((heads * rows, n), F32)
    fetch_gain.wait()
    fetch_wb.wait()
    gain = gain_ref[...]
    wb = wb_ref[...].astype(F32)
    wb = jnp.concatenate([jnp.broadcast_to(wb[h : h + 1], (rows, chan)) for h in range(heads)], 0)
    mine = [jnp.where(owner == k, wb, 0.0).astype(BF16) for k in range(rows)]
    mine = [jnp.concatenate(mine[k : k + 2], 1) for k in range(0, rows, 2)]
    for copy in fetches:
        copy.wait()
    for pair in range(rows // 2):
        both = [x_ref[k].astype(F32).reshape(peers, rows, chan) for k in (2 * pair, 2 * pair + 1)]
        out_ref[:, 2 * rows * pair : 2 * rows * (pair + 1), :] = jnp.concatenate(both, 1).astype(BF16)
    store(0, base)
    two = [jnp.concatenate([x_ref[k], x_ref[k + 1]], 1) for k in range(0, rows, 2)]
    normed = [layer_norm(values, centre, gain) for values in two]
    for pair in range(rows // 2):
        bias = bias + dot_nt(mine[pair], jnp.concatenate(normed[pair], 1))
    bias = bias.astype(BF16)
    for t in range(n // LANES):
        block = bias[:, t * LANES : (t + 1) * LANES]
        for d in range(peers):
            part = block[(d % 2) * half : (d % 2 + 1) * half]
            out_ref[d, base + t * half : base + (t + 1) * half] = part
    store(base, (n // LANES) * half)
    for copy in stores:
        copy.wait()


def prepare_kernel(
    heads, rows,
    chain_ref, mask_ref, cb_ref, w_ref, db_ref, gain_ref, wo_ref, wd_ref,
    term_ref, wt_ref, wk_out, dbc_ref, gain_out, wo_out, wd_out, swap_ref, centre_ref,
):
    gain_out[...] = gain_ref[...]
    swap_ref[...] = swap_matrix(rows)
    centre_ref[...] = centring(w_ref.shape[0])
    chan = w_ref.shape[0]
    width = wo_ref.shape[0]
    wk_out[...] = jnp.zeros_like(wk_out)
    wo_out[...] = jnp.zeros_like(wo_out)
    for side in range(2):
        wo_out[side * width : (side + 1) * width, side * chan : (side + 1) * chan] = wo_ref[...]
    wd_out[...] = wd_ref[...]
    n = chain_ref.shape[1]
    tiles = n // LANES
    dim = w_ref.shape[2] // 4

    def column_of(row):
        return jnp.transpose(jnp.broadcast_to(row, (LANES, LANES)))

    for kt in range(tiles):
        ks = slice(kt * LANES, (kt + 1) * LANES)
        chain_k = column_of(chain_ref[:, ks].astype(F32))
        mask_k = (column_of(mask_ref[:, ks].astype(F32)) - 1.0) * 1000000000.0
        for it in range(tiles):
            cs = slice(it * LANES, (it + 1) * LANES)
            same = chain_k == chain_ref[:, cs].astype(F32)
            for h in range(heads):
                term_ref[h, ks, cs] = (jnp.where(same, cb_ref[1, h], cb_ref[0, h]) + mask_k) * LOG2E
    for h in range(heads):
        turned = jnp.transpose(w_ref[:, h, :].astype(F32)).astype(BF16)
        for place, kind in enumerate((0, 2, 3)):
            start = place * width + h * dim
            wt_ref[start : start + dim] = turned[kind * dim : (kind + 1) * dim]
        for side in range(2):
            start = side * width + h * dim
            wk_out[start : start + dim, side * chan : (side + 1) * chan] = turned[dim : 2 * dim]
    bins = dbc_ref.shape[0]
    db_rows = jnp.broadcast_to(jnp.concatenate([db_ref[...], db_ref[...]], 1)[:, :LANES], (LANES, LANES))
    dbc_ref[...] = jnp.transpose(db_rows)[:bins]


def permuted(blocks, swap):
    left, right = jnp.concatenate(blocks[:2], 0), jnp.concatenate(blocks[2:], 0)
    return dot_nn(swap, jnp.concatenate([left, right], 1)).astype(BF16)


def project_kernel(heads, recv_ref, gain_ref, w_ref, wk_ref, swap_ref, centre_ref, x_s, spread_s, k_s, v_s, g_s, n_s):
    peers = recv_ref.shape[0]
    rows, n, chan = x_s.shape
    tiles = n // LANES
    dim = w_ref.shape[0] // (3 * heads)
    width = heads * dim
    base = rows * rows
    gain = gain_ref[...]
    swap = swap_ref[...]
    centre = centre_ref[...]
    group = 2 * rows
    w_k = wk_ref[...]

    quads = range(peers // 4)
    x = [permuted([recv_ref[4 * quad + s, :base] for s in range(4)], swap) for quad in quads]
    normed = [layer_norm(two, centre, gain) for two in x]
    keys = [dot_nt(jnp.concatenate(two, 1), w_k).astype(BF16) for two in normed]
    for quad in quads:
        for side in range(2):
            at = slice((2 * quad + side) * group, (2 * quad + side + 1) * group)
            x_s[:, at, :] = x[quad][:, side * chan : (side + 1) * chan].reshape(rows, group, chan)
            n_s[:, at, :] = normed[quad][side].reshape(rows, group, chan)
            k_s[:, at, :] = keys[quad][:, side * width : (side + 1) * width].reshape(rows, group, width)

    w_qvg = w_ref[...]
    zero = jnp.zeros((dim, LANES), BF16)

    def project(pair):
        both = dot_nt(w_qvg, n_s[pl.ds(2 * pair, 2)].reshape(2 * n, chan)).astype(BF16)
        for side in range(2):
            j = 2 * pair + side
            qvg = both[:, side * n : (side + 1) * n]
            v_s[j] = qvg[width : 2 * width]
            g_s[j] = jax.nn.sigmoid(qvg[2 * width :].astype(F32))
            for t in range(tiles):
                for h in range(heads):
                    for other in range(heads):
                        block = qvg[h * dim : (h + 1) * dim, t * LANES : (t + 1) * LANES] if h == other else zero
                        spread_s[j, t, other * dim : (other + 1) * dim, h * LANES : (h + 1) * LANES] = block

    if tiles == 1:
        for pair in range(rows // 2):
            project(pair)
    else:
        pl.loop(0, rows // 2)(project)


def attend_kernel(
    heads, fused,
    recv_ref, other_ref, term_ref, wo_ref, wd_ref, db_ref, x_s, spread_s, k_s, v_s, g_s,
    out_ref, *refs,
):
    if fused:
        second_ref, bias_s, inv_s, e_s, gated_s, new_s = refs
    else:
        bias_s, inv_s, e_s, gated_s = refs
    peers = recv_ref.shape[0]
    rows, n, chan = x_s.shape
    tiles = n // LANES
    dim = wo_ref.shape[0] // (2 * heads)
    half = heads // 2
    base = rows * rows
    core = lax.axis_index("row") % 2

    for s in range(peers):
        at = slice(s * rows, (s + 1) * rows)
        for block, owner in ((recv_ref[s, base:], core), (other_ref[s], 1 - core)):
            extra = block.astype(F32) * LOG2E
            for t in range(tiles):
                cs = slice(t * LANES, (t + 1) * LANES)
                for h in range(half):
                    start = (t * half + h) * rows
                    head = owner * half + h
                    bias_s[head, at, cs] = extra[start : start + rows] + term_ref[head, at, cs]

    scaling = dim ** (-0.5) * LOG2E
    w_out = wo_ref[...]

    def soften(j, t):
        cs = slice(t * LANES, (t + 1) * LANES)
        scores = dot_nn(k_s[j], spread_s[j, t])
        for h in range(heads):
            s = scores[:, h * LANES : (h + 1) * LANES] * scaling + bias_s[h, :, cs]
            e = jnp.exp2(s - jnp.max(s, 0, keepdims=True))
            inv_s[j, t, h : h + 1] = 1.0 / jnp.sum(e, 0, keepdims=True)
            e_s[j, t, :, h * LANES : (h + 1) * LANES] = e.astype(BF16)

    def combine(j, t):
        cs = slice(t * LANES, (t + 1) * LANES)
        for first in range(0, heads, 2):
            o = dot_nn(v_s[j, first * dim : (first + 2) * dim], e_s[j, t, :, first * LANES : (first + 2) * LANES])
            for side in range(2):
                h = first + side
                part = o[side * dim : (side + 1) * dim, side * LANES : (side + 1) * LANES]
                mine = slice(h * dim, (h + 1) * dim)
                gated_s[j, mine, cs] = (g_s[j, mine, cs] * (part * inv_s[j, t, h : h + 1])).astype(BF16)

    def updated(pair):
        both = gated_s[pl.ds(2 * pair, 2)].reshape(2 * heads * dim, n)
        return dot_tn(both, w_out).astype(BF16)

    if not fused:

        @pl.loop(0, rows // 2)
        def _(pair):
            for j in (2 * pair, 2 * pair + 1):
                for t in range(tiles):
                    soften(j, t)
                    combine(j, t)
            update = updated(pair)
            for side in range(2):
                out_ref[2 * pair + side] = update[:, side * chan : (side + 1) * chan]

        return

    for stage in (soften, combine):
        for j in range(rows):
            for t in range(tiles):
                stage(j, t)
    for j in range(0, rows, 2):
        update = updated(j // 2).astype(F32)
        both = []
        for side in range(2):
            new = (x_s[j + side].astype(F32) + update[:, side * chan : (side + 1) * chan]).astype(BF16)
            new_s[j + side] = new
            both.append(new.astype(F32).reshape(peers, rows, chan))
        out_ref[:, j * rows : (j + 2) * rows, :] = jnp.concatenate(both, 1).astype(BF16)
    logits_of(new_s, wd_ref[...], db_ref[:, :1], second_ref)


def logits_of(new_ref, w_dist, d_bias, out_ref):
    rows, n, chan = new_ref.shape
    logits = dot_nt(w_dist, new_ref[...].reshape(rows * n, chan)) + d_bias
    for j in range(rows):
        out_ref[j] = logits[:, j * n : (j + 1) * n].astype(BF16)


def finish_kernel(recv_ref, mirror_ref, wd_ref, db_ref, swap_ref, new_hbm, dist_hbm, new_ref, dist_ref, sems):
    peers, _, chan = recv_ref.shape
    rows = new_ref.shape[0]
    group = 2 * rows
    swap = swap_ref[...]
    for quad in range(peers // 4):
        new = permuted([recv_ref[4 * quad + s] for s in range(4)], swap)
        for side in range(2):
            at = slice((2 * quad + side) * group, (2 * quad + side + 1) * group)
            new_ref[:, at, :] = new[:, side * chan : (side + 1) * chan].reshape(rows, group, chan)
    copies = [pltpu.make_async_copy(new_ref, new_hbm, sems.at[0])]
    copies[0].start()
    logits_of(new_ref, wd_ref[...], db_ref[:, :1], dist_ref)
    for i in range(rows):
        dist_ref[i] = (dist_ref[i].astype(F32) + mirror_ref[i].astype(F32)).astype(BF16)
        if i % 2:
            at = pl.ds(i - 1, 2)
            copies.append(pltpu.make_async_copy(dist_ref.at[at], dist_hbm.at[at], sems.at[1 + i // 2]))
            copies[-1].start()
    for copy in copies:
        copy.wait()


def call(kernel, outs, args, scratch=(), smem=(), hbm=(), hbm_outs=False, limit=48):
    spaces = [pltpu.SMEM if i in smem else pl.ANY if i in hbm else pltpu.VMEM for i in range(len(args))]
    return pl.pallas_call(
        kernel,
        out_shape=[jax.ShapeDtypeStruct(s, d) for s, d in outs],
        in_specs=[pl.BlockSpec(memory_space=space) for space in spaces],
        out_specs=[pl.BlockSpec(memory_space=pl.ANY if hbm_outs else pltpu.VMEM)] * len(outs),
        scratch_shapes=list(scratch),
        compiler_params=pltpu.CompilerParams(vmem_limit_bytes=limit * 1024 * 1024),
    )(*args)


def swap_cores(values):
    peers = lax.axis_size("row")
    return lax.ppermute(values, "row", [(i, i ^ 1) for i in range(peers)])


def all_to_all(blocks):
    return lax.all_to_all(blocks, "row", split_axis=0, concat_axis=0, tiled=True)


def shards(
    pair_act, chain_id, residue_mask, norm_gain, w_proj, w_bias, chain_bias, w_out, w_dist, dist_bias,
):
    rows, n, chan = pair_act.shape
    peers = n // rows
    heads, dim = w_out.shape[0], w_out.shape[1]
    bins = w_dist.shape[1]
    tiles = n // LANES
    width = heads * dim
    fused = lax.axis_size("head") == 1
    gain = norm_gain[None, :]
    base = rows * rows
    length = base + tiles * heads * rows // 2

    (packed,) = call(
        pack_kernel,
        [((peers, length, chan), BF16)],
        [pair_act, gain, w_bias.T],
        scratch=[
            pltpu.VMEM(pair_act.shape, BF16),
            pltpu.VMEM(gain.shape, F32),
            pltpu.VMEM((heads, chan), BF16),
            pltpu.VMEM((peers, length, chan), BF16),
            pltpu.SemaphoreType.DMA((rows + 2,)),
            pltpu.SemaphoreType.DMA((2,)),
        ],
        hbm=(0, 1, 2),
        hbm_outs=True,
        limit=60,
    )
    received = all_to_all(packed)
    prepared = call(
        functools.partial(prepare_kernel, heads, rows),
        [
            ((heads, n, n), F32), ((3 * width, chan), BF16), ((2 * width, 2 * chan), BF16), ((bins, LANES), F32),
            ((1, chan), F32), ((2 * width, 2 * chan), BF16), ((bins, chan), BF16),
            ((2 * base, 2 * base), BF16), ((2 * chan, 2 * chan), BF16),
        ],
        [
            chain_id[None, :], residue_mask[None, :], chain_bias, w_proj, dist_bias[None, :],
            gain, w_out.reshape(width, chan), w_dist.T,
        ],
        smem=(2,),
    )
    received, *prepared = lax.optimization_barrier((received, *prepared))
    term, w_types, w_keys, db_col, gain, w_out, wd_t, swap, centre = prepared
    other_bias = swap_cores(received[:, base:])
    x_cols, spread, keys, values, gates = call(
        functools.partial(project_kernel, heads),
        [
            ((rows, n, chan), BF16),
            ((rows, tiles, width, heads * LANES), BF16),
            ((rows, n, width), BF16),
            ((rows, width, n), BF16),
            ((rows, width, n), F32),
        ],
        [received, gain, w_types, w_keys, swap, centre],
        scratch=[pltpu.VMEM((rows, n, chan), BF16)],
    )
    if fused:
        outs = [((peers, base, chan), BF16), ((rows, bins, n), BF16)]
    else:
        outs = [((rows, n, chan), BF16)]
    result = call(
        functools.partial(attend_kernel, heads, fused),
        outs,
        [received, other_bias, term, w_out, wd_t, db_col, x_cols, spread, keys, values, gates],
        scratch=[
            pltpu.VMEM((heads, n, n), F32),
            pltpu.VMEM((rows, tiles, heads, LANES), F32),
            pltpu.VMEM((rows, tiles, n, heads * LANES), BF16),
            pltpu.VMEM((rows, width, n), BF16),
        ]
        + [pltpu.VMEM((rows, n, chan), BF16)] * fused,
    )
    if fused:
        to_rows, mirror = result
    else:
        update = lax.psum(result[0], "head").astype(F32)
        new = (x_cols.astype(F32) + update).astype(BF16)
        logits = jnp.einsum("cb,jic->jbi", w_dist, new, preferred_element_type=F32)
        mirror = (logits + dist_bias[None, :, None]).astype(BF16)
        to_rows = new.reshape(rows, peers, rows, chan).transpose(1, 0, 2, 3).reshape(peers, base, chan)
    arrived = all_to_all(to_rows)
    new_rows, dist = call(
        finish_kernel,
        [((rows, n, chan), BF16), ((rows, bins, n), BF16)],
        [arrived, mirror, wd_t, db_col, swap],
        scratch=[
            pltpu.VMEM((rows, n, chan), BF16),
            pltpu.VMEM((rows, bins, n), BF16),
            pltpu.SemaphoreType.DMA((1 + rows // 2,)),
        ],
        hbm_outs=True,
    )
    return new_rows, dist.transpose(0, 2, 1)


def solution(mesh):
    in_specs = (
        P(("dp", "row"), None, None),
        P("dp"),
        P("dp"),
        P(),
        P(None, "head", None),
        P(None, "head"),
        P(None, "head"),
        P("head", None, None),
        P(),
        P(),
    )
    out_specs = (P(("dp", "row"), None, None), P(("dp", "row"), None, None))
    return jax.shard_map(shards, mesh=mesh, in_specs=in_specs, out_specs=out_specs, check_vma=False)
```

profile of v0, /device:TPU:0, one launch (start us, length us, event | category | flops | bytes accessed | tf_op | source)
XLA Modules:
  0.0 38.5 jit_solution(13739855470788922119)
XLA Ops:
  0.6 2.2 %shard_map.113 = bf16[16,80,128]{2,1,0:T(8,128)(2,1)} custom-call(bf16[8,128,128]{2,1,0:T(8,128)(2,1)} %x_hbm.1, f32[1,128]{1,0:T(1,128)} %bitcast.10, bf16[4,128]{1,0:T(4,128)(2,1)} %bitcast.15), custom_call_target="tpu_custom_call" | custom-call | tf_op jit(solution)/shard_map/pallas_call | solution.py:315
  2.8 0.0 copy-start
  2.8 0.0 copy-start.1
  2.8 0.0 copy-start.2
  2.8 0.0 copy-start.5
  2.8 0.0 copy-start.6
  2.8 0.0 copy-start.7
  2.9 7.5 %all-to-all-start = ((bf16[16,80,128]{2,1,0:T(8,128)(2,1)}), bf16[16,80,128]{2,1,0:T(8,128)(2,1)S(1)}, u32[]{:S(2)}, u32[]{:S(2)}) async-start(bf16[16,80,128]{2,1,0:T(8,128)(2,1)} %shard_map.113), calls=%async_computation | async-start | bytes 655360 | tf_op jit(solution)/shard_map/all_to_all | solution.py:331
  10.4 0.0 copy-start.3
  10.4 0.0 copy-start.4
  10.4 0.0 copy-done
  10.4 0.0 copy-done.1
  10.4 0.0 copy-done.2
  10.5 0.0 copy-done.5
  10.5 0.6 %copy-done.3 = f32[128]{0:T(128)S(1)} copy-done((f32[128]{0:T(128)S(1)}, f32[128]{0:T(128)}, u32[]{:S(2)}) %copy-start.3) | copy-done | bytes 536
  11.1 0.0 copy-done.4
  11.1 0.9 %shard_map.114 = (f32[4,128,128]{2,1,0:T(8,128)S(1)}, bf16[384,128]{1,0:T(8,128)(2,1)S(1)}, bf16[256,256]{1,0:T(8,128)(2,1)S(1)}, f32[64,128]{1,0:T(8,128)S(1)},...) custom-call(s32[1,128]{1,0:T(1,128)S(1)} %bitcast.12, ...), custom_call_target="tpu_custom_call" | custom-call | tf_op jit(solution)/shard_map/pallas_call | solution.py:315
  12.0 9.5 %all-to-all-done.recv_ref = bf16[16,80,128]{2,1,0:T(8,128)(2,1)S(1)} async-done(((bf16[16,80,128]{2,1,0:T(8,128)(2,1)}), bf16[16,80,128]{2,1,0:T(8,128)(2,1)S(1)}, u32[]{:S(2)}, u32[]{:S(2)}) %all-to-all-start) | async-done | bytes 327712 | tf_op jit(solution)/shard_map/all_to_all | solution.py:331
  21.5 0.1 collective-permute-start
  21.6 0.9 %shard_map.115 = (bf16[8,128,128]{2,1,0:T(8,128)(2,1)S(1)}, bf16[8,1,128,512]{3,2,1,0:T(8,128)(2,1)S(1)}, bf16[8,128,128]{2,1,0:T(8,128)(2,1)S(1)}, bf16[8,128,128]{2,1,0:T(8,128)(2,1)S(1)}, f32[8,128,128]{2,1,0:T(8,128)S(1)}) custom-call(bf16[16,80,128]{2,1,0:T(8,128)(2,1)S(1)} %all-to-all-done.recv_ref, f32[1,128]{1,0:T(1,128)S(1)} %get-tuple-element.44.gain_ref, ...), custom_call_target="tpu_custom_call" | custom-call | tf_op jit(solution)/shard_map/pallas_call | solution.py:315
  22.5 0.2 collective-permute-done.other_ref
  22.8 1.5 %shard_map.116 = (bf16[16,64,128]{2,1,0:T(8,128)(2,1)S(1)}, bf16[8,64,128]{2,1,0:T(8,128)(2,1)S(1)}) custom-call(bf16[16,80,128]{2,1,0:T(8,128)(2,1)S(1)} %all-to-all-done.recv_ref, bf16[16,16,128]{2,1,0:T(8,128)(2,1)S(1)} %collective-permute-done.other_ref, f32[4,128,128]{2,1,0:T(8,128)S(1)} %get-tuple-element.40.term_ref, ...), custom_call_target="tpu_custom_call" | custom-call | tf_op jit(solution)/shard_map/pallas_call | solution.py:315
  24.3 13.1 %all_to_all.10.recv_ref = bf16[16,64,128]{2,1,0:T(8,128)(2,1)S(1)} all-to-all(bf16[16,64,128]{2,1,0:T(8,128)(2,1)S(1)} %get-tuple-element.54), channel_id=1, replica_groups=mesh['dp'=2,'head'=1,'row'=16] {'row'}, dimensions={0} | all-to-all | bytes 524288 | tf_op jit(solution)/shard_map/all_to_all | solution.py:331
  37.4 1.1 %shard_map.117 = (bf16[8,128,128]{2,1,0:T(8,128)(2,1)}, bf16[8,64,128]{2,1,0:T(8,128)(2,1)}) custom-call(bf16[16,64,128]{2,1,0:T(8,128)(2,1)S(1)} %all_to_all.10.recv_ref, bf16[8,64,128]{2,1,0:T(8,128)(2,1)S(1)} %get-tuple-element.55.mirror_ref, bf16[64,128]{1,0:T(8,128)(2,1)S(1)} %get-tuple-element.42.wd_ref, f32[64,128]{1,0:T(8,128)S(1)} %get-tuple-element.43.db_ref, ...), custom_call_target="tpu_custom_call" | custom-call | tf_op jit(solution)/shard_map/pallas_call | solution.py:315
  (3 shorter events, 0.0 us)
Async XLA Ops:
  2.8 7.6 %copy-start = (bf16[128,4,128]{2,1,0:T(4,128)(2,1)S(1)}, bf16[128,4,128]{2,1,0:T(4,128)(2,1)}, u32[]{:S(2)}) copy-start(bf16[128,4,128]{2,1,0:T(4,128)(2,1)} %w_ref.1) | copy-start | bytes 393220
  2.8 7.6 %copy-start.1 = (bf16[4,32,128]{2,1,0:T(8,128)(2,1)S(1)}, bf16[4,32,128]{2,1,0:T(8,128)(2,1)}, u32[]{:S(2)}) copy-start(bf16[4,32,128]{2,1,0:T(8,128)(2,1)} %param.17) | copy-start | bytes 98308
  2.8 7.6 %copy-start.2 = (bf16[128,64]{0,1:T(8,128)(2,1)S(1)}, bf16[128,64]{0,1:T(8,128)(2,1)}, u32[]{:S(2)}) copy-start(bf16[128,64]{0,1:T(8,128)(2,1)} %param.18) | copy-start | bytes 49156
  2.8 7.6 %copy-start.5 = (s32[128]{0:T(128)S(1)}, s32[128]{0:T(128)}, u32[]{:S(2)}) copy-start(s32[128]{0:T(128)} %param.11) | copy-start | bytes 1540
  2.8 7.6 %copy-start.6 = (s32[128]{0:T(128)S(1)}, s32[128]{0:T(128)}, u32[]{:S(2)}) copy-start(s32[128]{0:T(128)} %param.12) | copy-start | bytes 1540
  2.8 7.6 %copy-start.7 = (f32[64]{0:T(128)S(1)}, f32[64]{0:T(128)}, u32[]{:S(2)}) copy-start(f32[64]{0:T(128)} %param.19) | copy-start | bytes 772
  2.9 18.6 %all-to-all-start = ((bf16[16,80,128]{2,1,0:T(8,128)(2,1)}), bf16[16,80,128]{2,1,0:T(8,128)(2,1)S(1)}, u32[]{:S(2)}, u32[]{:S(2)}) async-start(bf16[16,80,128]{2,1,0:T(8,128)(2,1)} %shard_map.113), calls=%async_computation | async-start | bytes 655360 | tf_op jit(solution)/shard_map/all_to_all | solution.py:331
  10.4 0.7 %copy-start.3 = (f32[128]{0:T(128)S(1)}, f32[128]{0:T(128)}, u32[]{:S(2)}) copy-start(f32[128]{0:T(128)} %param.13) | copy-start | bytes 1540
  10.4 0.7 %copy-start.4 = (f32[2,4]{1,0:T(2,128)S(1)}, f32[2,4]{1,0:T(2,128)}, u32[]{:S(2)}) copy-start(f32[2,4]{1,0:T(2,128)} %cb_ref.1) | copy-start | bytes 100
  21.5 1.3 %collective-permute-start = (bf16[16,16,128]{2,1,0:T(8,128)(2,1)S(1)}, bf16[16,16,128]{2,1,0:T(8,128)(2,1)S(1)}, u32[]{:S(2)}, u32[]{:S(2)}) collective-permute-start(bf16[16,16,128]{2,1,0:T(8,128)(2,1)S(1)} %slice.3), channel_id=1, source_target_pairs={{0,1},{1,0},{2,3},{3,2},{4,5},{5,4},{6,7},{7,6},{8,9},{9,8},{10,11... | collective-permute-start | bytes 196616 | tf_op jit(solution)/shard_map/ppermute | solution.py:327
where the time goes:
time: 38.8 us; the launch traced here: 38.5 us
  blocking collectives  13.1 us (34%)
  waiting for transfers between devices  9.73 us (25%)
  starting transfers between devices  7.64 us (20%)
  Pallas kernels  6.59 us (17%)
  between operations  0.78 us (2%)
  local copies, waits for them, and re-layouts  0.66 us (2%)
    all_to_all x1, blocking collectives, all_to_all(): lax.all_to_all(blocks, 'row', split_axis=0, concat_axis=0, tiled=True)  13.1 us
    all_to_all x1, waiting for transfers between devices, all_to_all(): lax.all_to_all(blocks, 'row', split_axis=0, concat_axis=0, tiled=True)  9.49 us
    all_to_all x1, starting transfers between devices, all_to_all(): lax.all_to_all(blocks, 'row', split_axis=0, concat_axis=0, tiled=True)  7.53 us
    pallas_call x5, Pallas kernels, call(): pl.pallas_call(kernel, out_shape=[jax.ShapeDtypeStruct(s, d) for s, d in...  6.59 us
  transfers between devices with their start and end apart: 2, of which 2 were waited for; matrix products, arithmetic and copies ran while one was open for 0% of the time, Pallas kernels for 5%

commit v1 on v0

--- a/solution.py
+++ b/solution.py
@@ -64,9 +64,8 @@
         copy.start()
     stores = []
 
-    def store(first, count):
-        at = pl.ds(first, count)
-        copy = pltpu.make_async_copy(out_ref.at[:, at, :], out_hbm.at[:, at, :], out_sems.at[len(stores)])
+    def store(*at):
+        copy = pltpu.make_async_copy(out_ref.at[at], out_hbm.at[at], out_sems.at[len(stores)])
         copy.start()
         stores.append(copy)
 
@@ -82,10 +81,14 @@
     mine = [jnp.concatenate(mine[k : k + 2], 1) for k in range(0, rows, 2)]
     for copy in fetches:
         copy.wait()
-    for pair in range(rows // 2):
-        both = [x_ref[k].astype(F32).reshape(peers, rows, chan) for k in (2 * pair, 2 * pair + 1)]
-        out_ref[:, 2 * rows * pair : 2 * rows * (pair + 1), :] = jnp.concatenate(both, 1).astype(BF16)
-    store(0, base)
+    share = peers // 4
+    for first in range(0, peers, share):
+        for pair in range(rows // 2):
+            at = pl.ds(first * rows, share * rows)
+            both = [x_ref[k, at, :].astype(F32).reshape(share, rows, chan) for k in (2 * pair, 2 * pair + 1)]
+            joined = jnp.concatenate(both, 1).astype(BF16)
+            out_ref[first : first + share, 2 * rows * pair : 2 * rows * (pair + 1), :] = joined
+        store(pl.ds(first, share), pl.ds(0, base), slice(None))
     two = [jnp.concatenate([x_ref[k], x_ref[k + 1]], 1) for k in range(0, rows, 2)]
     normed = [layer_norm(values, centre, gain) for values in two]
     for pair in range(rows // 2):
@@ -96,7 +99,7 @@
         for d in range(peers):
             part = block[(d % 2) * half : (d % 2 + 1) * half]
             out_ref[d, base + t * half : base + (t + 1) * half] = part
-    store(base, (n // LANES) * half)
+    store(slice(None), pl.ds(base, (n // LANES) * half), slice(None))
     for copy in stores:
         copy.wait()
 
@@ -150,7 +153,23 @@
     return dot_nn(swap, jnp.concatenate([left, right], 1)).astype(BF16)
 
 
-def project_kernel(heads, recv_ref, gain_ref, w_ref, wk_ref, swap_ref, centre_ref, x_s, spread_s, k_s, v_s, g_s, n_s):
+def unpack_bias(blocks, term_ref, owner, bias_ref):
+    half, n = bias_ref.shape[0], bias_ref.shape[1]
+    rows = n // len(blocks)
+    for s, block in enumerate(blocks):
+        at = slice(s * rows, (s + 1) * rows)
+        extra = block.astype(F32) * LOG2E
+        for t in range(n // LANES):
+            cs = slice(t * LANES, (t + 1) * LANES)
+            for h in range(half):
+                start = (t * half + h) * rows
+                bias_ref[h, at, cs] = extra[start : start + rows] + term_ref[owner * half + h, at, cs]
+
+
+def project_kernel(
+    heads, recv_ref, gain_ref, w_ref, wk_ref, swap_ref, centre_ref, term_ref,
+    x_s, spread_s, k_s, v_s, g_s, own_s, n_s,
+):
     peers = recv_ref.shape[0]
     rows, n, chan = x_s.shape
     tiles = n // LANES
@@ -195,35 +214,28 @@
             project(pair)
     else:
         pl.loop(0, rows // 2)(project)
+    unpack_bias([recv_ref[s, base:] for s in range(peers)], term_ref, lax.axis_index("row") % 2, own_s)
 
 
 def attend_kernel(
     heads, fused,
-    recv_ref, other_ref, term_ref, wo_ref, wd_ref, db_ref, x_s, spread_s, k_s, v_s, g_s,
+    other_ref, own_s, term_ref, wo_ref, wd_ref, db_ref, x_s, spread_s, k_s, v_s, g_s,
     out_ref, *refs,
 ):
     if fused:
         second_ref, bias_s, inv_s, e_s, gated_s, new_s = refs
     else:
         bias_s, inv_s, e_s, gated_s = refs
-    peers = recv_ref.shape[0]
+    peers = other_ref.shape[0]
     rows, n, chan = x_s.shape
     tiles = n // LANES
     dim = wo_ref.shape[0] // (2 * heads)
     half = heads // 2
-    base = rows * rows
     core = lax.axis_index("row") % 2
 
-    for s in range(peers):
-        at = slice(s * rows, (s + 1) * rows)
-        for block, owner in ((recv_ref[s, base:], core), (other_ref[s], 1 - core)):
-            extra = block.astype(F32) * LOG2E
-            for t in range(tiles):
-                cs = slice(t * LANES, (t + 1) * LANES)
-                for h in range(half):
-                    start = (t * half + h) * rows
-                    head = owner * half + h
-                    bias_s[head, at, cs] = extra[start : start + rows] + term_ref[head, at, cs]
+    bias_s[pl.ds(core * half, half)] = own_s[...]
+    other_half = bias_s.at[pl.ds((1 - core) * half, half)]
+    unpack_bias([other_ref[s] for s in range(peers)], term_ref, 1 - core, other_half)
 
     scaling = dim ** (-0.5) * LOG2E
     w_out = wo_ref[...]
@@ -292,19 +304,21 @@
     rows = new_ref.shape[0]
     group = 2 * rows
     swap = swap_ref[...]
+    copies = []
     for quad in range(peers // 4):
         new = permuted([recv_ref[4 * quad + s] for s in range(4)], swap)
         for side in range(2):
             at = slice((2 * quad + side) * group, (2 * quad + side + 1) * group)
             new_ref[:, at, :] = new[:, side * chan : (side + 1) * chan].reshape(rows, group, chan)
-    copies = [pltpu.make_async_copy(new_ref, new_hbm, sems.at[0])]
-    copies[0].start()
+        at = pl.ds(2 * quad * group, 2 * group)
+        copies.append(pltpu.make_async_copy(new_ref.at[:, at, :], new_hbm.at[:, at, :], sems.at[quad]))
+        copies[-1].start()
     logits_of(new_ref, wd_ref[...], db_ref[:, :1], dist_ref)
     for i in range(rows):
         dist_ref[i] = (dist_ref[i].astype(F32) + mirror_ref[i].astype(F32)).astype(BF16)
         if i % 2:
             at = pl.ds(i - 1, 2)
-            copies.append(pltpu.make_async_copy(dist_ref.at[at], dist_hbm.at[at], sems.at[1 + i // 2]))
+            copies.append(pltpu.make_async_copy(dist_ref.at[at], dist_hbm.at[at], sems.at[peers // 4 + i // 2]))
             copies[-1].start()
     for copy in copies:
         copy.wait()
@@ -355,7 +369,7 @@
             pltpu.VMEM((heads, chan), BF16),
             pltpu.VMEM((peers, length, chan), BF16),
             pltpu.SemaphoreType.DMA((rows + 2,)),
-            pltpu.SemaphoreType.DMA((2,)),
+            pltpu.SemaphoreType.DMA((5,)),
         ],
         hbm=(0, 1, 2),
         hbm_outs=True,
@@ -378,7 +392,7 @@
     received, *prepared = lax.optimization_barrier((received, *prepared))
     term, w_types, w_keys, db_col, gain, w_out, wd_t, swap, centre = prepared
     other_bias = swap_cores(received[:, base:])
-    x_cols, spread, keys, values, gates = call(
+    x_cols, spread, keys, values, gates, own_bias = call(
         functools.partial(project_kernel, heads),
         [
             ((rows, n, chan), BF16),
@@ -386,8 +400,9 @@
             ((rows, n, width), BF16),
             ((rows, width, n), BF16),
             ((rows, width, n), F32),
+            ((heads // 2, n, n), F32),
         ],
-        [received, gain, w_types, w_keys, swap, centre],
+        [received, gain, w_types, w_keys, swap, centre, term],
         scratch=[pltpu.VMEM((rows, n, chan), BF16)],
     )
     if fused:
@@ -397,7 +412,7 @@
     result = call(
         functools.partial(attend_kernel, heads, fused),
         outs,
-        [received, other_bias, term, w_out, wd_t, db_col, x_cols, spread, keys, values, gates],
+        [other_bias, own_bias, term, w_out, wd_t, db_col, x_cols, spread, keys, values, gates],
         scratch=[
             pltpu.VMEM((heads, n, n), F32),
             pltpu.VMEM((rows, tiles, heads, LANES), F32),
@@ -422,7 +437,7 @@
         scratch=[
             pltpu.VMEM((rows, n, chan), BF16),
             pltpu.VMEM((rows, bins, n), BF16),
-            pltpu.SemaphoreType.DMA((1 + rows // 2,)),
+            pltpu.SemaphoreType.DMA((peers // 4 + rows // 2,)),
         ],
         hbm_outs=True,
     )

time: 38.8 us -> 38.9 us (level)
  no operation moved by 1% of the time
where the time goes in v1:
time: 38.9 us; the launch traced here: 38.6 us
  blocking collectives  13.1 us (34%)
  waiting for transfers between devices  9.73 us (25%)
  starting transfers between devices  7.64 us (20%)
  Pallas kernels  6.66 us (17%)
  between operations  0.78 us (2%)
  local copies, waits for them, and re-layouts  0.66 us (2%)
    all_to_all x1, blocking collectives, all_to_all(): lax.all_to_all(blocks, 'row', split_axis=0, concat_axis=0, tiled=True)  13.1 us
    all_to_all x1, waiting for transfers between devices, all_to_all(): lax.all_to_all(blocks, 'row', split_axis=0, concat_axis=0, tiled=True)  9.49 us
    all_to_all x1, starting transfers between devices, all_to_all(): lax.all_to_all(blocks, 'row', split_axis=0, concat_axis=0, tiled=True)  7.53 us
    pallas_call x5, Pallas kernels, call(): pl.pallas_call(kernel, out_shape=[jax.ShapeDtypeStruct(s, d) for s, d in...  6.66 us
  transfers between devices with their start and end apart: 2, of which 2 were waited for; matrix products, arithmetic and copies ran while one was open for 0% of the time, Pallas kernels for 5%

profile of v1, /device:TPU:0, one launch (start us, length us, event | category | flops | bytes accessed | tf_op | source)
XLA Modules:
  0.0 38.6 jit_solution(17172411829917248188)
XLA Ops:
  0.6 2.2 %shard_map.113 = bf16[16,80,128]{2,1,0:T(8,128)(2,1)} custom-call(bf16[8,128,128]{2,1,0:T(8,128)(2,1)} %x_hbm.1, f32[1,128]{1,0:T(1,128)} %bitcast.10, bf16[4,128]{1,0:T(4,128)(2,1)} %bitcast.15), custom_call_target="tpu_custom_call" | custom-call | tf_op jit(solution)/shard_map/pallas_call | solution.py:329
  2.8 0.0 copy-start
  2.8 0.0 copy-start.1
  2.8 0.0 copy-start.2
  2.9 0.0 copy-start.5
  2.9 0.0 copy-start.6
  2.9 0.0 copy-start.7
  2.9 7.5 %all-to-all-start = ((bf16[16,80,128]{2,1,0:T(8,128)(2,1)}), bf16[16,80,128]{2,1,0:T(8,128)(2,1)S(1)}, u32[]{:S(2)}, u32[]{:S(2)}) async-start(bf16[16,80,128]{2,1,0:T(8,128)(2,1)} %shard_map.113), calls=%async_computation | async-start | bytes 655360 | tf_op jit(solution)/shard_map/all_to_all | solution.py:345
  10.4 0.0 copy-start.3
  10.4 0.0 copy-start.4
  10.4 0.0 copy-done
  10.5 0.0 copy-done.1
  10.5 0.0 copy-done.2
  10.5 0.0 copy-done.5
  10.5 0.6 %copy-done.3 = f32[128]{0:T(128)S(1)} copy-done((f32[128]{0:T(128)S(1)}, f32[128]{0:T(128)}, u32[]{:S(2)}) %copy-start.3) | copy-done | bytes 536
  11.1 0.0 copy-done.4
  11.1 0.9 %shard_map.114 = (f32[4,128,128]{2,1,0:T(8,128)S(1)}, bf16[384,128]{1,0:T(8,128)(2,1)S(1)}, bf16[256,256]{1,0:T(8,128)(2,1)S(1)}, f32[64,128]{1,0:T(8,128)S(1)},...) custom-call(s32[1,128]{1,0:T(1,128)S(1)} %bitcast.12, ...), custom_call_target="tpu_custom_call" | custom-call | tf_op jit(solution)/shard_map/pallas_call | solution.py:329
  12.0 9.5 %all-to-all-done.recv_ref = bf16[16,80,128]{2,1,0:T(8,128)(2,1)S(1)} async-done(((bf16[16,80,128]{2,1,0:T(8,128)(2,1)}), bf16[16,80,128]{2,1,0:T(8,128)(2,1)S(1)}, u32[]{:S(2)}, u32[]{:S(2)}) %all-to-all-start) | async-done | bytes 327712 | tf_op jit(solution)/shard_map/all_to_all | solution.py:345
  21.5 0.1 collective-permute-start
  21.6 0.9 %shard_map.115 = (bf16[8,128,128]{2,1,0:T(8,128)(2,1)S(1)}, bf16[8,1,128,512]{3,2,1,0:T(8,128)(2,1)S(1)}, bf16[8,128,128]{2,1,0:T(8,128)(2,1)S(1)}, bf16[8,128,1...) custom-call(bf16[16,80,128]{2,1,0:T(8,128)(2,1)S(1)} %all-to-all-done.recv_ref, ...), custom_call_target="tpu_custom_call" | custom-call | tf_op jit(solution)/shard_map/pallas_call | solution.py:329
  22.5 0.2 collective-permute-done.other_ref
  22.8 1.5 %shard_map.116 = (bf16[16,64,128]{2,1,0:T(8,128)(2,1)S(1)}, bf16[8,64,128]{2,1,0:T(8,128)(2,1)S(1)}) custom-call(bf16[16,16,128]{2,1,0:T(8,128)(2,1)S(1)} %collective-permute-done.other_ref, f32[2,128,128]{2,1,0:T(8,128)S(1)} %get-tuple-element.47.own_s, f32[4,128,128]{2,1,0:T(8,128)S(1)} %get-tuple-element.46.term_ref, ...), custom_call_target="tpu_custom_call" | custom-call | tf_op jit(solution)/shard_map/pallas_call | solution.py:329
  24.3 13.1 %all_to_all.10.recv_ref = bf16[16,64,128]{2,1,0:T(8,128)(2,1)S(1)} all-to-all(bf16[16,64,128]{2,1,0:T(8,128)(2,1)S(1)} %get-tuple-element.56), channel_id=1, replica_groups=mesh['dp'=2,'head'=1,'row'=16] {'row'}, dimensions={0} | all-to-all | bytes 524288 | tf_op jit(solution)/shard_map/all_to_all | solution.py:345
  37.4 1.1 %shard_map.117 = (bf16[8,128,128]{2,1,0:T(8,128)(2,1)}, bf16[8,64,128]{2,1,0:T(8,128)(2,1)}) custom-call(bf16[16,64,128]{2,1,0:T(8,128)(2,1)S(1)} %all_to_all.10.recv_ref, bf16[8,64,128]{2,1,0:T(8,128)(2,1)S(1)} %get-tuple-element.57.mirror_ref, bf16[64,128]{1,0:T(8,128)(2,1)S(1)} %get-tuple-element.49.wd_ref, f32[64,128]{1,0:T(8,128)S(1)} %get-tuple-element.50.db_ref, ...), custom_call_target="tpu_custom_call" | custom-call | tf_op jit(solution)/shard_map/pallas_call | solution.py:329
  (3 shorter events, 0.0 us)
Async XLA Ops:
  2.8 7.6 %copy-start = (bf16[128,4,128]{2,1,0:T(4,128)(2,1)S(1)}, bf16[128,4,128]{2,1,0:T(4,128)(2,1)}, u32[]{:S(2)}) copy-start(bf16[128,4,128]{2,1,0:T(4,128)(2,1)} %w_ref.1) | copy-start | bytes 393220
  2.8 7.6 %copy-start.1 = (bf16[4,32,128]{2,1,0:T(8,128)(2,1)S(1)}, bf16[4,32,128]{2,1,0:T(8,128)(2,1)}, u32[]{:S(2)}) copy-start(bf16[4,32,128]{2,1,0:T(8,128)(2,1)} %param.17) | copy-start | bytes 98308
  2.8 7.6 %copy-start.2 = (bf16[128,64]{0,1:T(8,128)(2,1)S(1)}, bf16[128,64]{0,1:T(8,128)(2,1)}, u32[]{:S(2)}) copy-start(bf16[128,64]{0,1:T(8,128)(2,1)} %param.18) | copy-start | bytes 49156
  2.9 7.6 %copy-start.5 = (s32[128]{0:T(128)S(1)}, s32[128]{0:T(128)}, u32[]{:S(2)}) copy-start(s32[128]{0:T(128)} %param.11) | copy-start | bytes 1540
  2.9 7.6 %copy-start.6 = (s32[128]{0:T(128)S(1)}, s32[128]{0:T(128)}, u32[]{:S(2)}) copy-start(s32[128]{0:T(128)} %param.12) | copy-start | bytes 1540
  2.9 7.6 %copy-start.7 = (f32[64]{0:T(128)S(1)}, f32[64]{0:T(128)}, u32[]{:S(2)}) copy-start(f32[64]{0:T(128)} %param.19) | copy-start | bytes 772
  2.9 18.6 %all-to-all-start = ((bf16[16,80,128]{2,1,0:T(8,128)(2,1)}), bf16[16,80,128]{2,1,0:T(8,128)(2,1)S(1)}, u32[]{:S(2)}, u32[]{:S(2)}) async-start(bf16[16,80,128]{2,1,0:T(8,128)(2,1)} %shard_map.113), calls=%async_computation | async-start | bytes 655360 | tf_op jit(solution)/shard_map/all_to_all | solution.py:345
  10.4 0.7 %copy-start.3 = (f32[128]{0:T(128)S(1)}, f32[128]{0:T(128)}, u32[]{:S(2)}) copy-start(f32[128]{0:T(128)} %param.13) | copy-start | bytes 1540
  10.4 0.7 %copy-start.4 = (f32[2,4]{1,0:T(2,128)S(1)}, f32[2,4]{1,0:T(2,128)}, u32[]{:S(2)}) copy-start(f32[2,4]{1,0:T(2,128)} %cb_ref.1) | copy-start | bytes 100
  21.5 1.3 %collective-permute-start = (bf16[16,16,128]{2,1,0:T(8,128)(2,1)S(1)}, bf16[16,16,128]{2,1,0:T(8,128)(2,1)S(1)}, u32[]{:S(2)}, u32[]{:S(2)}) collective-permute-start(bf16[16,16,128]{2,1,0:T(8,128)(2,1)S(1)} %slice.3), channel_id=1, source_target_pairs={{0,1},{1,0},{2,3},{3,2},{4,5},{5,4},{6,7},{7,6},{8,9},{9,8},{10,11... | collective-permute-start | bytes 196616 | tf_op jit(solution)/shard_map/ppermute | solution.py:341
